TPU v7x, 32 devices: a whole 2x2x4 slice. The times are simulated.
32 devices in a mesh: section: 8 (over y, x, core), rep: 4 (over z).
Axes of the slice: x: 2, y: 2, z: 4, core: 2. Of those that a mesh axis runs over, the one named last changes fastest.
Arguments:
- features: bfloat16 [8, 128, 2048], P(None, 'rep'), may hold values from -6 to 6
- positions: int32 [8, 128], P(None, 'rep'), may hold values from 0 to 63
- labels: int32 [8, 128], P(None, 'rep'), may hold values 0 or 1
- cross_u: bfloat16 [2, 8, 2048, 256], P(None, 'section'), may hold values from -0.125 to 0.125
- cross_v: bfloat16 [2, 8, 256, 2048], P(None, 'section'), may hold values from -0.1875 to 0.1875
- cross_bias: float32 [2, 8, 2048], P(None, 'section'), may hold values from -2 to 2
- head: float32 [2048], replicated, may hold values from -0.125 to 0.125
- pos_table: float32 [64, 256], replicated, may hold values from -6 to 6
- debias_hidden_weight: float32 [256, 256], replicated, may hold values from -0.375 to 0.375
- debias_tower_bias: float32 [256], replicated, may hold values from -3 to 3
- debias_output_weight: float32 [256], replicated, may hold values from -0.375 to 0.375
Outputs:
- loss: float32 [], replicated
- grad_u: float32 [2, 8, 2048, 256], P(None, 'section')
- grad_v: float32 [2, 8, 256, 2048], P(None, 'section')
- grad_bias: float32 [2, 8, 2048], P(None, 'section')
All inputs are finite; a program needn't handle non-finite values. No bound on the sum of `labels` on one device may be relied on, other than what follows from the above.
Results may differ from a plain program's by a relative error of at most 0.04.
Values may be sent and summed in bfloat16 or wider, within the bound.
A program may use at most 128 MiB of HBM per device.

v0:
```python
import jax
import jax.numpy as jnp
from jax import lax
from jax.sharding import PartitionSpec as P

EPS = 1e-05


def from_behind(value, axis, by):
    size = lax.axis_size(axis)
    return lax.ppermute(value, axis, [(i, (i + by) % size) for i in range(size)])


def layer_parts(x, x0, w_up, w_down, shift):
    xf = x.astype(jnp.float32)
    scale = lax.rsqrt(jnp.mean(xf * xf, axis=-1, keepdims=True) + EPS)
    normed = (xf * scale).astype(jnp.bfloat16)
    inner = jnp.dot(normed, w_up, preferred_element_type=jnp.float32).astype(jnp.bfloat16)
    cross = jnp.dot(inner, w_down, preferred_element_type=jnp.float32) + shift
    output = (xf + x0.astype(jnp.float32) * cross).astype(jnp.bfloat16)
    return (xf, scale, normed, inner, output)


def layer_back(grad_out, x0, xf, scale, normed, inner, w_up, w_down):
    gcross = (grad_out.astype(jnp.float32) * x0.astype(jnp.float32)).astype(jnp.bfloat16)
    gshift = jnp.sum(gcross.astype(jnp.float32), axis=0)
    gdown = jnp.einsum("br,bd->rd", inner, gcross, preferred_element_type=jnp.float32)
    ginner = jnp.einsum("bd,rd->br", gcross, w_down, preferred_element_type=jnp.float32).astype(
        jnp.bfloat16
    )
    gup = jnp.einsum("bd,br->dr", normed, ginner, preferred_element_type=jnp.float32)
    gnormed = jnp.einsum("br,dr->bd", ginner, w_up, preferred_element_type=jnp.float32)
    gin = (
        grad_out.astype(jnp.float32)
        + scale * gnormed
        - xf * scale**3 * jnp.mean(gnormed * xf, axis=-1, keepdims=True)
    )
    return (gin.astype(jnp.bfloat16), gup, gdown, gshift)


def local(
    features,
    positions,
    labels,
    cross_u,
    cross_v,
    cross_bias,
    head,
    pos_table,
    debias_hidden_weight,
    debias_tower_bias,
    debias_output_weight,
):
    w_up = cross_u[:, 0]
    w_down = cross_v[:, 0]
    shifts = cross_bias[:, 0]
    sections = lax.axis_size("section")
    replicas = lax.axis_size("rep")
    section = lax.axis_index("section")
    micro = features.shape[0]
    rows = features.shape[1]
    width = features.shape[2]
    loops = w_up.shape[0]
    depth = loops * sections
    ticks = depth + micro - 1
    hidden_index = lax.Precision.HIGHEST

    def bounds(slot, member):
        live = (member < micro) & (slot >= 0) & (slot < loops)
        return (live, jnp.clip(slot, 0, loops - 1), jnp.clip(member, 0, micro - 1))

    def forward_tick(tick, carry):
        state, stash, finals = carry
        delta = tick - section
        live, slot, member = bounds(jnp.floor_divide(delta, sections), jnp.mod(delta, sections))
        fresh = features[member]
        inject = (section == 0) & (tick < micro)
        x_in = jnp.where(inject, fresh, state)
        stash = stash.at[slot, member].set(jnp.where(live, x_in, stash[slot, member]))
        output = layer_parts(x_in, fresh, w_up[slot], w_down[slot], shifts[slot])[4]
        output = jnp.where(live, output, jnp.zeros_like(output))
        finished = live & (slot == loops - 1) & (section == sections - 1)
        finals = finals.at[member].set(jnp.where(finished, output, finals[member]))
        state = from_behind(output, "section", 1)
        return (state, stash, finals)

    start = (
        jnp.zeros((rows, width), jnp.bfloat16),
        jnp.zeros((loops, micro, rows, width), jnp.bfloat16),
        jnp.zeros((micro, rows, width), jnp.bfloat16),
    )
    unused_state, stash, finals = lax.fori_loop(0, ticks, forward_tick, start)
    total = micro * rows * replicas
    onehot = (positions[..., None] == jnp.arange(pos_table.shape[0], dtype=jnp.int32)).astype(
        jnp.float32
    )
    embedded_rows = jnp.einsum("mbp,pt->mbt", onehot, pos_table, precision=hidden_index)
    hidden_state = jax.nn.relu(
        jnp.einsum("sxf,fh->sxh", embedded_rows, debias_hidden_weight, precision=hidden_index)
        + debias_tower_bias
    )
    click_logit = jnp.einsum("mbd,d->mb", finals.astype(jnp.float32), head, precision=hidden_index)
    click_logit = click_logit + jnp.einsum(
        "dpf,f->dp", hidden_state, debias_output_weight, precision=hidden_index
    )
    labf = labels.astype(jnp.float32)
    loss_part = jnp.sum(jax.nn.softplus(click_logit) - labf * click_logit)
    dlogit = (jax.nn.sigmoid(click_logit) - labf) / total
    dfinal = (dlogit[..., None] * head).astype(jnp.bfloat16)
    is_last = section == sections - 1
    loss = lax.psum(jnp.where(is_last, loss_part, 0.0), ("section", "rep")) / total

    def backward_tick(tick, carry):
        grad_state, grad_up, grad_down, grad_shift = carry
        delta = tick + section + 1 - depth
        live, slot, member = bounds(-jnp.floor_divide(delta, sections), jnp.mod(delta, sections))
        inject = is_last & (tick < micro)
        grad_in = jnp.where(inject, dfinal[member], grad_state)
        fresh = features[member]
        saved = stash[slot, member]
        xf, scale, normed, inner, unused = layer_parts(
            saved, fresh, w_up[slot], w_down[slot], shifts[slot]
        )
        gin, gup, gdown, gshift = layer_back(
            grad_in, fresh, xf, scale, normed, inner, w_up[slot], w_down[slot]
        )
        gin = jnp.where(live, gin, jnp.zeros_like(gin))
        gup = jnp.where(live, gup, 0.0)
        gdown = jnp.where(live, gdown, 0.0)
        gshift = jnp.where(live, gshift, 0.0)
        grad_up = grad_up.at[slot].add(gup)
        grad_down = grad_down.at[slot].add(gdown)
        grad_shift = grad_shift.at[slot].add(gshift)
        grad_state = from_behind(gin, "section", -1)
        return (grad_state, grad_up, grad_down, grad_shift)

    begin = (
        jnp.zeros((rows, width), jnp.bfloat16),
        jnp.zeros(w_up.shape, jnp.float32),
        jnp.zeros(w_down.shape, jnp.float32),
        jnp.zeros(shifts.shape, jnp.float32),
    )
    unused_grad, grad_up, grad_down, grad_shift = lax.fori_loop(0, ticks, backward_tick, begin)
    grad_up, grad_down, grad_shift = lax.psum((grad_up, grad_down, grad_shift), "rep")
    return (loss, grad_up[:, None], grad_down[:, None], grad_shift[:, None])


def solution(mesh):
    return jax.shard_map(
        local,
        mesh=mesh,
        in_specs=(
            P(None, "rep", None),
            P(None, "rep"),
            P(None, "rep"),
            P(None, "section", None, None),
            P(None, "section", None, None),
            P(None, "section", None),
            P(),
            P(),
            P(),
            P(),
            P(),
        ),
        out_specs=(
            P(),
            P(None, "section", None, None),
            P(None, "section", None, None),
            P(None, "section", None),
        ),
        check_vma=False,
    )
```

profile of v0, /device:TPU:0, one launch (start us, length us, event | category | flops | bytes accessed | tf_op | source)
XLA Modules:
  0.0 1055.7 jit_solution(2716866033504771296)
XLA Ops:
  14.5 328.0 %while.47 = (s32[]{:T(128)}, bf16[32,2048]{1,0:T(8,128)(2,1)S(1)}, bf16[2,8,32,2048]{3,2,1,0:T(8,128)(2,1)}, bf16[8,32,2048]{2,1,0:T(8,128)(2,1)}, s32[]{:T(128)...) while((s32[]{:T(128)}, bf16[32,2048]{1,0:T(8,128)(2,1)S(1)}, ...), condition=%wide.region_4.5_spmd, body=%wide.region_0.4_spmd.sunk | while | flops 68296816 | bytes 4748254 | solution.py:92
  23.9 5.5 collective-permute-done
  38.4 5.3 collective-permute-done
  52.6 5.3 collective-permute-done
  66.9 5.3 collective-permute-done
  81.1 5.3 collective-permute-done
  95.3 5.3 collective-permute-done
  109.6 5.3 collective-permute-done
  123.8 5.3 collective-permute-done
  138.0 5.3 collective-permute-done
  152.3 5.3 collective-permute-done
  166.5 5.3 collective-permute-done
  180.7 5.3 collective-permute-done
  194.9 5.3 collective-permute-done
  209.2 5.3 collective-permute-done
  223.4 5.3 collective-permute-done
  237.6 5.3 collective-permute-done
  251.8 5.3 collective-permute-done
  323.0 5.3 collective-permute-done
  337.2 5.3 collective-permute-done
  352.5 394.3 %while.48 = (s32[]{:T(128)}, bf16[32,2048]{1,0:T(8,128)(2,1)S(1)}, f32[2,2048,256]{2,1,0:T(8,128)}, f32[2,256,2048]{2,1,0:T(8,128)}, f32[2,2048]{1,0:T(2,128)S(1...) while((s32[]{:T(128)}, bf16[32,2048]{1,0:T(8,128)(2,1)S(1)}, ...), condition=%wide.region_13.14_spmd, body=%wide.region_7.13_spmd.sunk | while | flops 172773536 | bytes 14409210 | solution.py:143
  747.4 44.5 %psum.28 = f32[]{:T(128)} all-reduce(f32[]{:T(128)S(6)} %select_n.313), channel_id=1, replica_groups=mesh['section'=8,'rep'=4] {'section','rep'}, use_global_device_ids=true, to_apply=%region_6.7 | all-reduce | flops 1 | bytes 8 | tf_op jit(solution)/shard_map/psum | solution.py:111
  792.6 20.3 %psum.31 = f32[2,1,2048]{2,1,0:T(1,128)} all-reduce(f32[2,1,2048]{2,1,0:T(1,128)S(1)} %broadcast_in_dim.98), channel_id=1, replica_groups=mesh['section'=8,'rep'=4] {'rep'}, use_global_device_ids=true, to_apply=%region_16.17 | all-reduce | flops 4096 | bytes 32768 | tf_op jit(solution)/shard_map/psum | solution.py:144
  812.9 228.2 %all-reduce.3.cloned.1.call-done = (f32[2,1,2048,256]{3,2,1,0:T(8,128)}, f32[2,1,256,2048]{3,2,1,0:T(8,128)}) async-done(((f32[2,1,2048,256]{3,2,1,0:T(8,128)}, f32[2,1,256,2048]{3,2,1,0:T(8,128)}), (f32[2,1,2048,256]{3,2,1,0:T(8,128)}, f32[2,1,256,2048]{3,2,1,0:T(8,128)})) %all-reduce.3.cloned.1.call-update) | async-done | bytes 8388624 | tf_op jit(solution)/shard_map/psum | solution.py:144
  (593 shorter events, 642.1 us)
Async XLA Ops:
  7.2 1033.9 %all-reduce.3.cloned.1.call-start = ((), (), s32[]{:S(2)}) async-start(), calls=%async_computation | async-start | bytes 16777216 | tf_op jit(solution)/shard_map/psum | solution.py:144
  357.7 11.2 %collective-permute-start.1 = (bf16[32,2048]{1,0:T(8,128)(2,1)S(1)}, bf16[32,2048]{1,0:T(8,128)(2,1)S(1)}, u32[]{:S(2)}, u32[]{:S(2)}) collective-permute-start(bf16[32,2048]{1,0:T(8,128)(2,1)S(1)} %fusion.115), channel_id=1, source_target_pairs={{0,28},{4,0},{8,4},{12,8},{16,12},{20,16},{24,20},{28,24},{1,29},{... | collective-permute-start | bytes 393224 | tf_op jit(solution)/shard_map/while/body/eval_jaxpr/ppermute | solution.py:11
  374.2 11.2 %collective-permute-start.1 = (bf16[32,2048]{1,0:T(8,128)(2,1)S(1)}, bf16[32,2048]{1,0:T(8,128)(2,1)S(1)}, u32[]{:S(2)}, u32[]{:S(2)}) collective-permute-start(bf16[32,2048]{1,0:T(8,128)(2,1)S(1)} %fusion.115), channel_id=1, source_target_pairs={{0,28},{4,0},{8,4},{12,8},{16,12},{20,16},{24,20},{28,24},{1,29},{... | collective-permute-start | bytes 393224 | tf_op jit(solution)/shard_map/while/body/eval_jaxpr/ppermute | solution.py:11
  390.8 11.2 %collective-permute-start.1 = (bf16[32,2048]{1,0:T(8,128)(2,1)S(1)}, bf16[32,2048]{1,0:T(8,128)(2,1)S(1)}, u32[]{:S(2)}, u32[]{:S(2)}) collective-permute-start(bf16[32,2048]{1,0:T(8,128)(2,1)S(1)} %fusion.115), channel_id=1, source_target_pairs={{0,28},{4,0},{8,4},{12,8},{16,12},{20,16},{24,20},{28,24},{1,29},{... | collective-permute-start | bytes 393224 | tf_op jit(solution)/shard_map/while/body/eval_jaxpr/ppermute | solution.py:11
  407.3 15.1 %collective-permute-start.1 = (bf16[32,2048]{1,0:T(8,128)(2,1)S(1)}, bf16[32,2048]{1,0:T(8,128)(2,1)S(1)}, u32[]{:S(2)}, u32[]{:S(2)}) collective-permute-start(bf16[32,2048]{1,0:T(8,128)(2,1)S(1)} %fusion.115), channel_id=1, source_target_pairs={{0,28},{4,0},{8,4},{12,8},{16,12},{20,16},{24,20},{28,24},{1,29},{... | collective-permute-start | bytes 393224 | tf_op jit(solution)/shard_map/while/body/eval_jaxpr/ppermute | solution.py:11
  427.7 11.2 %collective-permute-start.1 = (bf16[32,2048]{1,0:T(8,128)(2,1)S(1)}, bf16[32,2048]{1,0:T(8,128)(2,1)S(1)}, u32[]{:S(2)}, u32[]{:S(2)}) collective-permute-start(bf16[32,2048]{1,0:T(8,128)(2,1)S(1)} %fusion.115), channel_id=1, source_target_pairs={{0,28},{4,0},{8,4},{12,8},{16,12},{20,16},{24,20},{28,24},{1,29},{... | collective-permute-start | bytes 393224 | tf_op jit(solution)/shard_map/while/body/eval_jaxpr/ppermute | solution.py:11
  444.2 11.2 %collective-permute-start.1 = (bf16[32,2048]{1,0:T(8,128)(2,1)S(1)}, bf16[32,2048]{1,0:T(8,128)(2,1)S(1)}, u32[]{:S(2)}, u32[]{:S(2)}) collective-permute-start(bf16[32,2048]{1,0:T(8,128)(2,1)S(1)} %fusion.115), channel_id=1, source_target_pairs={{0,28},{4,0},{8,4},{12,8},{16,12},{20,16},{24,20},{28,24},{1,29},{... | collective-permute-start | bytes 393224 | tf_op jit(solution)/shard_map/while/body/eval_jaxpr/ppermute | solution.py:11
  460.7 11.2 %collective-permute-start.1 = (bf16[32,2048]{1,0:T(8,128)(2,1)S(1)}, bf16[32,2048]{1,0:T(8,128)(2,1)S(1)}, u32[]{:S(2)}, u32[]{:S(2)}) collective-permute-start(bf16[32,2048]{1,0:T(8,128)(2,1)S(1)} %fusion.115), channel_id=1, source_target_pairs={{0,28},{4,0},{8,4},{12,8},{16,12},{20,16},{24,20},{28,24},{1,29},{... | collective-permute-start | bytes 393224 | tf_op jit(solution)/shard_map/while/body/eval_jaxpr/ppermute | solution.py:11
  477.3 12.6 %collective-permute-start.1 = (bf16[32,2048]{1,0:T(8,128)(2,1)S(1)}, bf16[32,2048]{1,0:T(8,128)(2,1)S(1)}, u32[]{:S(2)}, u32[]{:S(2)}) collective-permute-start(bf16[32,2048]{1,0:T(8,128)(2,1)S(1)} %fusion.115), channel_id=1, source_target_pairs={{0,28},{4,0},{8,4},{12,8},{16,12},{20,16},{24,20},{28,24},{1,29},{... | collective-permute-start | bytes 393224 | tf_op jit(solution)/shard_map/while/body/eval_jaxpr/ppermute | solution.py:11
  495.2 11.2 %collective-permute-start.1 = (bf16[32,2048]{1,0:T(8,128)(2,1)S(1)}, bf16[32,2048]{1,0:T(8,128)(2,1)S(1)}, u32[]{:S(2)}, u32[]{:S(2)}) collective-permute-start(bf16[32,2048]{1,0:T(8,128)(2,1)S(1)} %fusion.115), channel_id=1, source_target_pairs={{0,28},{4,0},{8,4},{12,8},{16,12},{20,16},{24,20},{28,24},{1,29},{... | collective-permute-start | bytes 393224 | tf_op jit(solution)/shard_map/while/body/eval_jaxpr/ppermute | solution.py:11
  511.7 11.2 %collective-permute-start.1 = (bf16[32,2048]{1,0:T(8,128)(2,1)S(1)}, bf16[32,2048]{1,0:T(8,128)(2,1)S(1)}, u32[]{:S(2)}, u32[]{:S(2)}) collective-permute-start(bf16[32,2048]{1,0:T(8,128)(2,1)S(1)} %fusion.115), channel_id=1, source_target_pairs={{0,28},{4,0},{8,4},{12,8},{16,12},{20,16},{24,20},{28,24},{1,29},{... | collective-permute-start | bytes 393224 | tf_op jit(solution)/shard_map/while/body/eval_jaxpr/ppermute | solution.py:11
  528.2 11.2 %collective-permute-start.1 = (bf16[32,2048]{1,0:T(8,128)(2,1)S(1)}, bf16[32,2048]{1,0:T(8,128)(2,1)S(1)}, u32[]{:S(2)}, u32[]{:S(2)}) collective-permute-start(bf16[32,2048]{1,0:T(8,128)(2,1)S(1)} %fusion.115), channel_id=1, source_target_pairs={{0,28},{4,0},{8,4},{12,8},{16,12},{20,16},{24,20},{28,24},{1,29},{... | collective-permute-start | bytes 393224 | tf_op jit(solution)/shard_map/while/body/eval_jaxpr/ppermute | solution.py:11
  544.7 15.1 %collective-permute-start.1 = (bf16[32,2048]{1,0:T(8,128)(2,1)S(1)}, bf16[32,2048]{1,0:T(8,128)(2,1)S(1)}, u32[]{:S(2)}, u32[]{:S(2)}) collective-permute-start(bf16[32,2048]{1,0:T(8,128)(2,1)S(1)} %fusion.115), channel_id=1, source_target_pairs={{0,28},{4,0},{8,4},{12,8},{16,12},{20,16},{24,20},{28,24},{1,29},{... | collective-permute-start | bytes 393224 | tf_op jit(solution)/shard_map/while/body/eval_jaxpr/ppermute | solution.py:11
  565.1 11.2 %collective-permute-start.1 = (bf16[32,2048]{1,0:T(8,128)(2,1)S(1)}, bf16[32,2048]{1,0:T(8,128)(2,1)S(1)}, u32[]{:S(2)}, u32[]{:S(2)}) collective-permute-start(bf16[32,2048]{1,0:T(8,128)(2,1)S(1)} %fusion.115), channel_id=1, source_target_pairs={{0,28},{4,0},{8,4},{12,8},{16,12},{20,16},{24,20},{28,24},{1,29},{... | collective-permute-start | bytes 393224 | tf_op jit(solution)/shard_map/while/body/eval_jaxpr/ppermute | solution.py:11
  581.7 11.2 %collective-permute-start.1 = (bf16[32,2048]{1,0:T(8,128)(2,1)S(1)}, bf16[32,2048]{1,0:T(8,128)(2,1)S(1)}, u32[]{:S(2)}, u32[]{:S(2)}) collective-permute-start(bf16[32,2048]{1,0:T(8,128)(2,1)S(1)} %fusion.115), channel_id=1, source_target_pairs={{0,28},{4,0},{8,4},{12,8},{16,12},{20,16},{24,20},{28,24},{1,29},{... | collective-permute-start | bytes 393224 | tf_op jit(solution)/shard_map/while/body/eval_jaxpr/ppermute | solution.py:11
  598.2 11.2 %collective-permute-start.1 = (bf16[32,2048]{1,0:T(8,128)(2,1)S(1)}, bf16[32,2048]{1,0:T(8,128)(2,1)S(1)}, u32[]{:S(2)}, u32[]{:S(2)}) collective-permute-start(bf16[32,2048]{1,0:T(8,128)(2,1)S(1)} %fusion.115), channel_id=1, source_target_pairs={{0,28},{4,0},{8,4},{12,8},{16,12},{20,16},{24,20},{28,24},{1,29},{... | collective-permute-start | bytes 393224 | tf_op jit(solution)/shard_map/while/body/eval_jaxpr/ppermute | solution.py:11
  614.7 12.6 %collective-permute-start.1 = (bf16[32,2048]{1,0:T(8,128)(2,1)S(1)}, bf16[32,2048]{1,0:T(8,128)(2,1)S(1)}, u32[]{:S(2)}, u32[]{:S(2)}) collective-permute-start(bf16[32,2048]{1,0:T(8,128)(2,1)S(1)} %fusion.115), channel_id=1, source_target_pairs={{0,28},{4,0},{8,4},{12,8},{16,12},{20,16},{24,20},{28,24},{1,29},{... | collective-permute-start | bytes 393224 | tf_op jit(solution)/shard_map/while/body/eval_jaxpr/ppermute | solution.py:11
  632.6 11.2 %collective-permute-start.1 = (bf16[32,2048]{1,0:T(8,128)(2,1)S(1)}, bf16[32,2048]{1,0:T(8,128)(2,1)S(1)}, u32[]{:S(2)}, u32[]{:S(2)}) collective-permute-start(bf16[32,2048]{1,0:T(8,128)(2,1)S(1)} %fusion.115), channel_id=1, source_target_pairs={{0,28},{4,0},{8,4},{12,8},{16,12},{20,16},{24,20},{28,24},{1,29},{... | collective-permute-start | bytes 393224 | tf_op jit(solution)/shard_map/while/body/eval_jaxpr/ppermute | solution.py:11
  649.1 11.2 %collective-permute-start.1 = (bf16[32,2048]{1,0:T(8,128)(2,1)S(1)}, bf16[32,2048]{1,0:T(8,128)(2,1)S(1)}, u32[]{:S(2)}, u32[]{:S(2)}) collective-permute-start(bf16[32,2048]{1,0:T(8,128)(2,1)S(1)} %fusion.115), channel_id=1, source_target_pairs={{0,28},{4,0},{8,4},{12,8},{16,12},{20,16},{24,20},{28,24},{1,29},{... | collective-permute-start | bytes 393224 | tf_op jit(solution)/shard_map/while/body/eval_jaxpr/ppermute | solution.py:11
  665.6 11.2 %collective-permute-start.1 = (bf16[32,2048]{1,0:T(8,128)(2,1)S(1)}, bf16[32,2048]{1,0:T(8,128)(2,1)S(1)}, u32[]{:S(2)}, u32[]{:S(2)}) collective-permute-start(bf16[32,2048]{1,0:T(8,128)(2,1)S(1)} %fusion.115), channel_id=1, source_target_pairs={{0,28},{4,0},{8,4},{12,8},{16,12},{20,16},{24,20},{28,24},{1,29},{... | collective-permute-start | bytes 393224 | tf_op jit(solution)/shard_map/while/body/eval_jaxpr/ppermute | solution.py:11
  682.1 15.1 %collective-permute-start.1 = (bf16[32,2048]{1,0:T(8,128)(2,1)S(1)}, bf16[32,2048]{1,0:T(8,128)(2,1)S(1)}, u32[]{:S(2)}, u32[]{:S(2)}) collective-permute-start(bf16[32,2048]{1,0:T(8,128)(2,1)S(1)} %fusion.115), channel_id=1, source_target_pairs={{0,28},{4,0},{8,4},{12,8},{16,12},{20,16},{24,20},{28,24},{1,29},{... | collective-permute-start | bytes 393224 | tf_op jit(solution)/shard_map/while/body/eval_jaxpr/ppermute | solution.py:11
  702.6 11.2 %collective-permute-start.1 = (bf16[32,2048]{1,0:T(8,128)(2,1)S(1)}, bf16[32,2048]{1,0:T(8,128)(2,1)S(1)}, u32[]{:S(2)}, u32[]{:S(2)}) collective-permute-start(bf16[32,2048]{1,0:T(8,128)(2,1)S(1)} %fusion.115), channel_id=1, source_target_pairs={{0,28},{4,0},{8,4},{12,8},{16,12},{20,16},{24,20},{28,24},{1,29},{... | collective-permute-start | bytes 393224 | tf_op jit(solution)/shard_map/while/body/eval_jaxpr/ppermute | solution.py:11
  719.1 11.2 %collective-permute-start.1 = (bf16[32,2048]{1,0:T(8,128)(2,1)S(1)}, bf16[32,2048]{1,0:T(8,128)(2,1)S(1)}, u32[]{:S(2)}, u32[]{:S(2)}) collective-permute-start(bf16[32,2048]{1,0:T(8,128)(2,1)S(1)} %fusion.115), channel_id=1, source_target_pairs={{0,28},{4,0},{8,4},{12,8},{16,12},{20,16},{24,20},{28,24},{1,29},{... | collective-permute-start | bytes 393224 | tf_op jit(solution)/shard_map/while/body/eval_jaxpr/ppermute | solution.py:11
  735.6 11.2 %collective-permute-start.1 = (bf16[32,2048]{1,0:T(8,128)(2,1)S(1)}, bf16[32,2048]{1,0:T(8,128)(2,1)S(1)}, u32[]{:S(2)}, u32[]{:S(2)}) collective-permute-start(bf16[32,2048]{1,0:T(8,128)(2,1)S(1)} %fusion.115), channel_id=1, source_target_pairs={{0,28},{4,0},{8,4},{12,8},{16,12},{20,16},{24,20},{28,24},{1,29},{... | collective-permute-start | bytes 393224 | tf_op jit(solution)/shard_map/while/body/eval_jaxpr/ppermute | solution.py:11
  (32 other events, 808.9 us)
Sparse Core Ops, SparseCore 0:
  746.9 294.0 all-reduce.2
where the time goes:
time: 1060 us
  matrix products  357 us (34%)
  waiting for transfers between devices  350 us (33%)
  other arithmetic  188 us (18%)
  blocking collectives  64.9 us (6%)
  local copies, waits for them, and re-layouts  59.1 us (6%)
  starting transfers between devices  16.7 us (2%)
  between operations  16.5 us (2%)
    psum x1, waiting for transfers between devices, local(): lax.psum((grad_up, grad_down, grad_shift), 'rep')  228 us
    ppermute x46, waiting for transfers between devices, from_behind(): lax.ppermute(value, axis, [(i, (i + by) % size) for i in range(size)])  122 us
    dot_general x23, matrix products, layer_back(): jnp.einsum('br,bd->rd', inner, gcross, preferred_element_type=jnp.float32)  108 us
    dot_general x23, matrix products, layer_back(): jnp.einsum('bd,br->dr', normed, ginner, preferred_element_type=jnp.float32)  97.3 us
    another operation x115, other arithmetic  81.3 us
    dot_general x23, matrix products, layer_parts(): cross = jnp.dot(inner, w_down, preferred_element_type=jnp.float32) + shift  74.2 us
    scatter x23, other arithmetic, forward_tick(): stash.at[slot, member].set(jnp.where(live, x_in, stash[slot, member]))  51.4 us
    psum x1, blocking collectives, local(): lax.psum(jnp.where(is_last, loss_part, 0.0), ('section', 'rep')) / total  44.5 us
  transfers between devices with their start and end apart: 47, of which 24 were waited for; matrix products, arithmetic and copies ran while one was open for 24% of the time, Pallas kernels for 0%

commit v1 on v0

v1 whole, which is shorter than its diff:
```python
import functools

import jax
import jax.numpy as jnp
from jax import lax
from jax.experimental import pallas as pl
from jax.experimental.pallas import tpu as pltpu
from jax.sharding import PartitionSpec as P

EPS = 1e-05
MESH = pl.DeviceIdType.MESH
NN = (((1,), (0,)), ((), ()))
NT = (((1,), (1,)), ((), ()))
TN = (((0,), (0,)), ((), ()))


def dot(a, b, dims):
    return lax.dot_general(a, b, dims, preferred_element_type=jnp.float32)


def kernel(
    total,
    feat,
    pos,
    lab,
    u,
    v,
    bias,
    head,
    table,
    hidden_w,
    tower_b,
    out_w,
    gu,
    gv,
    gb,
    loss,
    xs,
    outs,
    normed,
    inner,
    scales,
    gs,
    gouts,
    gcross,
    ginner,
    tower,
    labcol,
    loss_rows,
    fsend,
    frecv,
    bsend,
    brecv,
):
    micro, rows, width = feat.shape
    loops = u.shape[0]
    sections = lax.axis_size("section")
    section = lax.axis_index("section")
    after = lax.rem(section + 1, sections)
    before = lax.rem(section + sections - 1, sections)
    is_first = section == 0
    is_last = section == sections - 1
    first = jnp.where(is_first, 1, 0)
    last = jnp.where(is_last, 1, 0)

    barrier = pltpu.get_barrier_semaphore()
    for neighbour in (before, after):
        pl.semaphore_signal(
            barrier, inc=1, device_id={"section": neighbour}, device_id_type=MESH
        )

    @pl.when(is_first)
    def _():
        xs[0] = feat[...]

    @pl.when(is_last)
    def _():
        hidden = jax.nn.relu(
            lax.dot_general(
                table[...],
                hidden_w[...],
                NN,
                precision=lax.Precision.HIGHEST,
                preferred_element_type=jnp.float32,
            )
            + tower_b[...]
        )
        by_pos = jnp.sum(hidden * out_w[...], axis=1, keepdims=True)
        places = by_pos.shape[0]
        square = (rows, rows)
        eye = lax.broadcasted_iota(jnp.int32, square, 0) == lax.broadcasted_iota(
            jnp.int32, square, 1
        )
        ids = lax.broadcasted_iota(jnp.int32, (places, rows), 0)
        for m in range(micro):
            row = jnp.sum(
                jnp.where(ids == pos[m : m + 1, :], by_pos, 0.0), axis=0, keepdims=True
            )
            tower[m] = jnp.sum(jnp.where(eye, row, 0.0), axis=1, keepdims=True)
            labf = lab[m : m + 1, :].astype(jnp.float32)
            labcol[m] = jnp.sum(jnp.where(eye, labf, 0.0), axis=1, keepdims=True)

    loss_rows[...] = jnp.zeros_like(loss_rows)
    pl.semaphore_wait(barrier, 2)

    def forward_copy(slot, m, to_slot):
        return pltpu.make_async_remote_copy(
            src_ref=outs.at[slot, m],
            dst_ref=xs.at[to_slot, m],
            send_sem=fsend.at[slot, m],
            recv_sem=frecv.at[to_slot, m],
            device_id={"section": after},
            device_id_type=MESH,
        )

    def backward_copy(slot, m, to_slot):
        return pltpu.make_async_remote_copy(
            src_ref=gouts.at[slot, m],
            dst_ref=gs.at[to_slot, m],
            send_sem=bsend.at[slot, m],
            recv_sem=brecv.at[to_slot, m],
            device_id={"section": before},
            device_id_type=MESH,
        )

    def rows_of(m):
        return pl.ds(pl.multiple_of(m * rows, rows), rows)

    def backward(slot, m):
        g = gs[slot, m].astype(jnp.float32)
        gc = (g * feat[m].astype(jnp.float32)).astype(jnp.bfloat16)
        gcross[slot, rows_of(m), :] = gc
        gi = dot(gc, v[slot, 0], NT).astype(jnp.bfloat16)
        ginner[slot, rows_of(m), :] = gi

        @pl.when(jnp.logical_not(is_first & (slot == 0)))
        def _():
            gn = dot(gi, u[slot, 0], NT)
            xf = xs[slot, m].astype(jnp.float32)
            scale = scales[slot, m]
            inside = jnp.mean(gn * xf, axis=-1, keepdims=True)
            gin = g + scale * gn - xf * (scale * scale * scale * inside)
            gouts[slot, m] = gin.astype(jnp.bfloat16)
            backward_copy(slot, m, slot - first).start()

    def forward(t, carry):
        slot, m = t // micro, t % micro

        @pl.when(jnp.logical_not(is_first & (slot == 0)))
        def _():
            forward_copy(slot, m, slot).wait_recv()

        xf = xs[slot, m].astype(jnp.float32)
        scale = lax.rsqrt(jnp.mean(xf * xf, axis=-1, keepdims=True) + EPS)
        scales[slot, m] = scale
        nm = (xf * scale).astype(jnp.bfloat16)
        normed[slot, rows_of(m), :] = nm
        mid = dot(nm, u[slot, 0], NN).astype(jnp.bfloat16)
        inner[slot, rows_of(m), :] = mid
        cross = dot(mid, v[slot, 0], NN) + bias[slot]
        out = (xf + feat[m].astype(jnp.float32) * cross).astype(jnp.bfloat16)
        ends = is_last & (slot == loops - 1)

        @pl.when(jnp.logical_not(ends))
        def _():
            outs[slot, m] = out
            forward_copy(slot, m, slot + last).start()

        @pl.when(ends)
        def _():
            logit = (
                jnp.sum(out.astype(jnp.float32) * head[...], axis=-1, keepdims=True)
                + tower[m]
            )
            labf = labcol[m]
            soft = jnp.maximum(logit, 0.0) + jnp.log1p(jnp.exp(-jnp.abs(logit)))
            loss_rows[...] += soft - labf * logit
            dlogit = (1.0 / (1.0 + jnp.exp(-logit)) - labf) / total
            gs[slot, m] = (dlogit * head[...]).astype(jnp.bfloat16)
            backward(slot, m)

        return carry

    lax.fori_loop(0, loops * micro, forward, 0)

    def weight_grads(slot):
        part = 512
        for c in range(width // part):
            cols = slice(c * part, (c + 1) * part)
            gu[slot, 0, cols, :] = dot(normed[slot, :, cols], ginner[slot], TN).astype(gu.dtype)
            gc = gcross[slot, :, cols]
            gv[slot, 0, :, cols] = dot(inner[slot], gc, TN).astype(gv.dtype)
            gb[slot, :, cols] = jnp.sum(gc.astype(jnp.float32), axis=0, keepdims=True)

    for back in range(loops):
        slot = loops - 1 - back

        def step(m, carry, slot=slot):
            ends = is_last & (slot == loops - 1)

            @pl.when(jnp.logical_not(ends))
            def _():
                backward_copy(slot, m, slot).wait_recv()
                backward(slot, m)

            return carry

        lax.fori_loop(0, micro, step, 0)
        weight_grads(slot)

    def drain(t, carry):
        slot, m = t // micro, t % micro

        @pl.when(jnp.logical_not(is_last & (slot == loops - 1)))
        def _():
            forward_copy(slot, m, slot).wait_send()

        @pl.when(jnp.logical_not(is_first & (slot == 0)))
        def _():
            backward_copy(slot, m, slot).wait_send()

        return carry

    lax.fori_loop(0, loops * micro, drain, 0)
    loss[...] = jnp.broadcast_to(jnp.sum(loss_rows[...], keepdims=True), loss.shape)


def local(
    features,
    positions,
    labels,
    cross_u,
    cross_v,
    cross_bias,
    head,
    pos_table,
    debias_hidden_weight,
    debias_tower_bias,
    debias_output_weight,
):
    micro, rows, width = features.shape
    loops, _, _, rank = cross_u.shape
    total = micro * rows * lax.axis_size("rep")
    bf16, f32 = jnp.bfloat16, jnp.float32
    vmem = pl.BlockSpec(memory_space=pltpu.VMEM)
    act = pltpu.VMEM((loops, micro, rows, width), bf16)
    wide = pltpu.VMEM((loops, micro * rows, width), bf16)
    thin = pltpu.VMEM((loops, micro * rows, rank), bf16)
    sems = pltpu.SemaphoreType.DMA((loops, micro))
    gu, gv, gb, loss = pl.pallas_call(
        functools.partial(kernel, float(total)),
        out_shape=(
            jax.ShapeDtypeStruct(cross_u.shape, bf16),
            jax.ShapeDtypeStruct(cross_v.shape, bf16),
            jax.ShapeDtypeStruct(cross_bias.shape, f32),
            jax.ShapeDtypeStruct((8, 128), f32),
        ),
        in_specs=[vmem] * 11,
        out_specs=(vmem,) * 4,
        scratch_shapes=[
            act,
            act,
            wide,
            thin,
            pltpu.VMEM((loops, micro, rows, 1), f32),
            act,
            act,
            wide,
            thin,
            pltpu.VMEM((micro, rows, 1), f32),
            pltpu.VMEM((micro, rows, 1), f32),
            pltpu.VMEM((rows, 1), f32),
            sems,
            sems,
            sems,
            sems,
        ],
        compiler_params=pltpu.CompilerParams(
            collective_id=0, has_side_effects=True, vmem_limit_bytes=56 * 2**20
        ),
    )(
        features,
        positions,
        labels,
        cross_u,
        cross_v,
        cross_bias,
        head[None, :],
        pos_table,
        debias_hidden_weight,
        debias_tower_bias[None, :],
        debias_output_weight[None, :],
    )
    loss = lax.psum(loss[0, 0], ("section", "rep")) / total
    gu, gv, gb = lax.psum((gu, gv, gb), "rep")
    return (loss, gu.astype(f32), gv.astype(f32), gb)


def solution(mesh):
    return jax.shard_map(
        local,
        mesh=mesh,
        in_specs=(
            P(None, "rep", None),
            P(None, "rep"),
            P(None, "rep"),
            P(None, "section", None, None),
            P(None, "section", None, None),
            P(None, "section", None),
            P(),
            P(),
            P(),
            P(),
            P(),
        ),
        out_specs=(
            P(),
            P(None, "section", None, None),
            P(None, "section", None, None),
            P(None, "section", None),
        ),
        check_vma=False,
    )
```

time: 1060 us -> 305 us (0.29)
  matrix products: 357 us -> 0 us
  waiting for transfers between devices: 350 us -> 89.6 us
  other arithmetic: 188 us -> 6.62 us
  Pallas kernels: 0 us -> 127 us
  local copies, waits for them, and re-layouts: 59.1 us -> 1.2 us
  starting transfers between devices: 16.7 us -> 0.04 us
    dot_general x119 -> x0, matrix products: 357 us -> none  [the longest x23 108 us: layer_back(): jnp.einsum('br,bd->rd', inner, gcross, preferred_element_type=jnp.float32)]
    psum x1, waiting for transfers between devices: 228 us -> 89.5 us  [local(): gu, gv, gb = lax.psum((gu, gv, gb), 'rep')]
    pallas_call x0 -> x1, Pallas kernels: none -> 127 us  [local(): pl.pallas_call(functools.partial(kernel, float(total)), out_shape=(jax.Sh...]
    ppermute x46 -> x0, waiting for transfers between devices: 122 us -> none  [from_behind(): lax.ppermute(value, axis, [(i, (i + by) % size) for i in range(size)])]
    another operation x115 -> x0, other arithmetic: 81.3 us -> none
    scatter x23 -> x0, other arithmetic: 51.4 us -> none  [forward_tick(): stash.at[slot, member].set(jnp.where(live, x_in, stash[slot, member]))]
    dynamic_slice x69 -> x0, local copies, waits for them, and re-layouts: 42.6 us -> none  [the longest x23 21.2 us: forward_tick(): stash[slot, member]]
    reduce_sum x46 -> x0, other arithmetic: 27.2 us -> none  [the longest x23 24.1 us: layer_back(): gshift = jnp.sum(gcross.astype(jnp.float32), axis=0)]
  transfers between devices with their start and end apart: 47 -> 1, of which waited for: 24 -> 1; matrix products, arithmetic and copies ran while one was open for 24% -> 0% of each run, Pallas kernels for 0% -> 0%
where the time goes in v1:
time: 305 us
  Pallas kernels  127 us (42%)
  waiting for transfers between devices  89.6 us (29%)
  blocking collectives  65 us (21%)
  between operations  15.8 us (5%)
  other arithmetic  6.62 us (2%)
    pallas_call x1, Pallas kernels, local(): pl.pallas_call(functools.partial(kernel, float(total)), out_shape=(jax.Sh...  127 us
    psum x1, waiting for transfers between devices, local(): gu, gv, gb = lax.psum((gu, gv, gb), 'rep')  89.5 us
    psum x1, blocking collectives, local(): loss = lax.psum(loss[0, 0], ('section', 'rep')) / total  43.3 us
    psum x1, blocking collectives, local(): gu, gv, gb = lax.psum((gu, gv, gb), 'rep')  21.7 us
    convert_element_type x2, other arithmetic, local(): return (loss, gu.astype(f32), gv.astype(f32), gb)  6.62 us
  transfers between devices with their start and end apart: 1, of which 1 were waited for; matrix products, arithmetic and copies ran while one was open for 0% of the time, Pallas kernels for 0%

profile of v1, /device:TPU:0, one launch (start us, length us, event | category | flops | bytes accessed | tf_op | source)
XLA Modules:
  0.0 305.0 jit_solution(14593497155818689846)
XLA Ops:
  7.2 0.0 all-reduce.3.cloned.1.call-start
  7.2 126.8 %shard_map.138 = (bf16[2,1,2048,256]{3,2,1,0:T(8,128)(2,1)}, bf16[2,1,256,2048]{3,2,1,0:T(8,128)(2,1)}, f32[2,1,2048]{2,1,0:T(1,128)}, f32[8,128]{1,0:T(8,128)}) custom-call(bf16[8,32,2048]{2,1,0:T(8,128)(2,1)} %feat.1, s32[8,32]{1,0:T(8,128)} %pos.1, s32[8,32]{1,0:T(8,128)} %lab.1, bf16[2,1,2048,256]{3,2,1,0:T(8,128)(2,1)} %u.1, ...), custom_call_target="tpu_custom_call" | custom-call | tf_op jit(solution)/shard_map/pallas_call | solution.py:250
  134.0 0.0 copy-start.1
  134.0 0.0 all-reduce.3.cloned.1.call-update
  134.0 1.2 slice.3
  135.2 43.3 %psum.28 = f32[]{:T(128)} all-reduce(f32[]{:T(128)} %bitcast.3), channel_id=1, replica_groups=mesh['section'=8,'rep'=4] {'section','rep'}, use_global_device_ids=true, to_apply=%region_0.0 | all-reduce | flops 1 | bytes 8 | tf_op jit(solution)/shard_map/psum | solution.py:294
  179.2 0.0 copy-done.1
  179.2 21.7 %psum.31 = f32[2,1,2048]{2,1,0:T(1,128)} all-reduce(f32[2,1,2048]{2,1,0:T(1,128)S(1)} %copy-done.1), channel_id=1, replica_groups=mesh['section'=8,'rep'=4] {'rep'}, use_global_device_ids=true, to_apply=%region_3.0 | all-reduce | flops 4096 | bytes 32768 | tf_op jit(solution)/shard_map/psum | solution.py:295
  200.9 89.5 %all-reduce.3.cloned.1.call-done = (bf16[2,1,2048,256]{3,2,1,0:T(8,128)(2,1)}, bf16[2,1,256,2048]{3,2,1,0:T(8,128)(2,1)}) async-done(((bf16[2,1,2048,256]{3,2,1,0:T(8,128)(2,1)}, bf16[2,1,256,2048]{3,2,1,0:T(8,128)(2,1)}), (bf16[2,1,2048,256]{3,2,1,0:T(8,128)(2,1)}, bf16[2,1,256,2048]{3,2,1,0:T(8,128)(2,1)})) %all-reduce.3.cloned.1.call-update) | async-done | bytes 4194320 | tf_op jit(solution)/shard_map/psum | solution.py:295
  290.4 0.0 copy-start
  290.4 4.1 %convert_element_type.6 = f32[2,1,2048,256]{3,2,1,0:T(8,128)} convert(bf16[2,1,2048,256]{3,2,1,0:T(8,128)(2,1)} %get-tuple-element.12) | non-fusion elementwise | flops 1048576 | bytes 6291456 | tf_op jit(solution)/shard_map/convert_element_type | solution.py:296
  294.5 0.0 copy-done
  294.5 2.5 convert_element_type.7
Async XLA Ops:
  7.2 283.3 %all-reduce.3.cloned.1.call-start = ((), (), s32[]{:S(2)}) async-start(), calls=%async_computation | async-start | bytes 8388608 | tf_op jit(solution)/shard_map/psum | solution.py:295
  134.0 45.2 %copy-start.1 = (f32[2,1,2048]{2,1,0:T(1,128)S(1)}, f32[2,1,2048]{2,1,0:T(1,128)}, u32[]{:S(2)}) copy-start(f32[2,1,2048]{2,1,0:T(1,128)} %get-tuple-element.11) | copy-start | bytes 49156
  290.4 4.1 %copy-start = (bf16[2,1,256,2048]{3,2,1,0:T(8,128)(2,1)S(1)}, bf16[2,1,256,2048]{3,2,1,0:T(8,128)(2,1)}, u32[]{:S(2)}) copy-start(bf16[2,1,256,2048]{3,2,1,0:T(8,128)(2,1)} %get-tuple-element.13) | copy-start | bytes 6291460
Sparse Core Ops, SparseCore 0:
  134.1 156.2 all-reduce.2

commit v2 on v1

--- a/solution.py
+++ b/solution.py
@@ -8,6 +8,7 @@
 from jax.sharding import PartitionSpec as P
 
 EPS = 1e-05
+PARTS = 16
 MESH = pl.DeviceIdType.MESH
 NN = (((1,), (0,)), ((), ()))
 NT = (((1,), (1,)), ((), ()))
@@ -51,6 +52,22 @@
     frecv,
     bsend,
     brecv,
+    own_u,
+    own_v,
+    part_u,
+    part_v,
+    inn_u,
+    inn_v,
+    asend,
+    precv,
+    osend,
+    irecv,
+    loss_in,
+    lsend,
+    lrecv,
+    small,
+    ssend,
+    srecv,
 ):
     micro, rows, width = feat.shape
     loops = u.shape[0]
@@ -68,6 +85,15 @@
         pl.semaphore_signal(
             barrier, inc=1, device_id={"section": neighbour}, device_id_type=MESH
         )
+    replicas = lax.axis_size("rep")
+    replica = lax.axis_index("rep")
+    for step in range(1, replicas):
+        pl.semaphore_signal(
+            barrier,
+            inc=1,
+            device_id={"rep": lax.rem(replica + step, replicas)},
+            device_id_type=MESH,
+        )
 
     @pl.when(is_first)
     def _():
@@ -101,7 +127,7 @@
             labcol[m] = jnp.sum(jnp.where(eye, labf, 0.0), axis=1, keepdims=True)
 
     loss_rows[...] = jnp.zeros_like(loss_rows)
-    pl.semaphore_wait(barrier, 2)
+    pl.semaphore_wait(barrier, 1 + replicas)
 
     def forward_copy(slot, m, to_slot):
         return pltpu.make_async_remote_copy(
@@ -183,19 +209,130 @@
 
     lax.fori_loop(0, loops * micro, forward, 0)
 
+    middle_left = (replicas - 1) // 2
+    middle_right = middle_left + 1
+    on_left = replica <= middle_left
+    in_middle = (replica == middle_left) | (replica == middle_right)
+    inward = jnp.where(on_left, replica + 1, replica - 1)
+    has_outward = (replica > 0) & (replica < replicas - 1)
+    outward = jnp.where(on_left, replica - 1, replica + 1)
+    outward = jnp.clip(outward, 0, replicas - 1)
+    pieces = loops * PARTS
+    rank = own_v.shape[1]
+    tall_u, tall_v = width // PARTS, rank // PARTS
+    lag = jnp.where(in_middle, 3, 5)
+
+    def piece(ref, kind, q):
+        tall = (tall_u, tall_v)[kind]
+        slot, p = loops - 1 - q // PARTS, q % PARTS
+        return ref.at[slot, pl.ds(pl.multiple_of(p * tall, tall), tall), :]
+
+    def rep_copy(kind, q, source, target, send, recv, to):
+        return pltpu.make_async_remote_copy(
+            src_ref=piece(source, kind, q),
+            dst_ref=piece(target, kind, q),
+            send_sem=send.at[kind, q],
+            recv_sem=recv.at[kind, q],
+            device_id={"rep": to},
+            device_id_type=MESH,
+        )
+
+    own, part, inn, done = (own_u, own_v), (part_u, part_v), (inn_u, inn_v), (gu, gv)
+
+    def to_middle(kind, q):
+        return rep_copy(kind, q, own[kind], part[kind], asend, precv, inward)
+
+    def across(kind, q):
+        return rep_copy(kind, q, own[kind], inn[kind], asend, irecv, inward)
+
+    def to_ends(kind, q):
+        return rep_copy(kind, q, done[kind], inn[kind], osend, irecv, outward)
+
+    def add(a, b):
+        return (a.astype(jnp.float32) + b.astype(jnp.float32)).astype(jnp.bfloat16)
+
+    def gather_in(q):
+        for kind in range(2):
+
+            @pl.when(has_outward)
+            def _(kind=kind):
+                to_middle(kind, q).wait_recv()
+                mine = piece(own[kind], kind, q)
+                mine[...] = add(mine[...], piece(part[kind], kind, q)[...])
+
+            @pl.when(in_middle)
+            def _(kind=kind):
+                across(kind, q).start()
+
+            @pl.when(jnp.logical_not(in_middle))
+            def _(kind=kind):
+                to_middle(kind, q).start()
+
+    def give_out(q):
+        for kind in range(2):
+            across(kind, q).wait_recv()
+            arrived = piece(inn[kind], kind, q)[...]
+            result = piece(done[kind], kind, q)
+
+            @pl.when(in_middle)
+            def _(kind=kind, arrived=arrived, result=result):
+                result[...] = add(piece(own[kind], kind, q)[...], arrived)
+
+            @pl.when(jnp.logical_not(in_middle))
+            def _(arrived=arrived, result=result):
+                result[...] = arrived
+
+            @pl.when(has_outward)
+            def _(kind=kind):
+                to_ends(kind, q).start()
+
+    def reduce_step(t):
+        @pl.when((t >= 1) & (t - 1 < pieces))
+        def _():
+            gather_in(t - 1)
+
+        @pl.when((t >= lag) & (t - lag < pieces))
+        def _():
+            give_out(t - lag)
+
     def weight_grads(slot):
         part = 512
         for c in range(width // part):
             cols = slice(c * part, (c + 1) * part)
-            gu[slot, 0, cols, :] = dot(normed[slot, :, cols], ginner[slot], TN).astype(gu.dtype)
+            own_u[slot, cols, :] = dot(normed[slot, :, cols], ginner[slot], TN).astype(
+                jnp.bfloat16
+            )
             gc = gcross[slot, :, cols]
-            gv[slot, 0, :, cols] = dot(inner[slot], gc, TN).astype(gv.dtype)
-            gb[slot, :, cols] = jnp.sum(gc.astype(jnp.float32), axis=0, keepdims=True)
-
+            own_v[slot, :, cols] = dot(inner[slot], gc, TN).astype(jnp.bfloat16)
+            small[replica, slot : slot + 1, cols] = jnp.sum(
+                gc.astype(jnp.float32), axis=0, keepdims=True
+            )
+
+    def loss_copy():
+        return pltpu.make_async_remote_copy(
+            src_ref=loss_in,
+            dst_ref=loss_in,
+            send_sem=lsend,
+            recv_sem=lrecv,
+            device_id={"section": before},
+            device_id_type=MESH,
+        )
+
+    def small_copy(source, to):
+        return pltpu.make_async_remote_copy(
+            src_ref=small.at[source],
+            dst_ref=small.at[source],
+            send_sem=ssend.at[to],
+            recv_sem=srecv.at[source],
+            device_id={"rep": to},
+            device_id_type=MESH,
+        )
+
+    beside = micro <= PARTS
     for back in range(loops):
         slot = loops - 1 - back
 
-        def step(m, carry, slot=slot):
+        def step(m, carry, slot=slot, back=back):
             ends = is_last & (slot == loops - 1)
 
             @pl.when(jnp.logical_not(ends))
@@ -203,10 +340,38 @@
                 backward_copy(slot, m, slot).wait_recv()
                 backward(slot, m)
 
+            if back > 0 and beside:
+                reduce_step((back - 1) * micro + m)
             return carry
 
         lax.fori_loop(0, micro, step, 0)
+        if back == 0:
+
+            @pl.when(is_last)
+            def _():
+                loss_in[...] = jnp.broadcast_to(
+                    jnp.sum(loss_rows[...], keepdims=True), loss_in.shape
+                )
+
+            @pl.when(jnp.logical_not(is_last))
+            def _():
+                loss_copy().wait_recv()
+
+            @pl.when(jnp.logical_not(is_first))
+            def _():
+                loss_copy().start()
+
         weight_grads(slot)
+
+    small[replica, loops : loops + 1, :] = jnp.broadcast_to(loss_in[:1, :1], (1, width))
+    for step in range(1, replicas):
+        small_copy(replica, lax.rem(replica + step, replicas)).start()
+
+    def tail(t, carry):
+        reduce_step(t)
+        return carry
+
+    lax.fori_loop((loops - 1) * micro if beside else 0, pieces + 5, tail, 0)
 
     def drain(t, carry):
         slot, m = t // micro, t % micro
@@ -222,7 +387,33 @@
         return carry
 
     lax.fori_loop(0, loops * micro, drain, 0)
-    loss[...] = jnp.broadcast_to(jnp.sum(loss_rows[...], keepdims=True), loss.shape)
+
+    def drain_rep(q, carry):
+        for kind in range(2):
+            across(kind, q).wait_send()
+
+            @pl.when(has_outward)
+            def _(kind=kind):
+                to_ends(kind, q).wait_send()
+
+        return carry
+
+    lax.fori_loop(0, pieces, drain_rep, 0)
+
+    @pl.when(jnp.logical_not(is_first))
+    def _():
+        loss_copy().wait_send()
+
+    for step in range(1, replicas):
+        other = lax.rem(replica + step, replicas)
+        small_copy(replica, other).wait_send()
+        small_copy(other, replica).wait_recv()
+    summed = small[0]
+    for r in range(1, replicas):
+        summed = summed + small[r]
+    for slot in range(loops):
+        gb[slot] = summed[slot : slot + 1, :]
+    loss[...] = summed[loops : loops + 1, :128] / total
 
 
 def local(
@@ -246,14 +437,18 @@
     act = pltpu.VMEM((loops, micro, rows, width), bf16)
     wide = pltpu.VMEM((loops, micro * rows, width), bf16)
     thin = pltpu.VMEM((loops, micro * rows, rank), bf16)
+    grad_u = pltpu.VMEM((loops, width, rank), bf16)
+    grad_v = pltpu.VMEM((loops, rank, width), bf16)
+    rep_sems = pltpu.SemaphoreType.DMA((2, loops * PARTS))
+    replicas = lax.axis_size("rep")
     sems = pltpu.SemaphoreType.DMA((loops, micro))
     gu, gv, gb, loss = pl.pallas_call(
         functools.partial(kernel, float(total)),
         out_shape=(
-            jax.ShapeDtypeStruct(cross_u.shape, bf16),
-            jax.ShapeDtypeStruct(cross_v.shape, bf16),
+            jax.ShapeDtypeStruct((loops, width, rank), bf16),
+            jax.ShapeDtypeStruct((loops, rank, width), bf16),
             jax.ShapeDtypeStruct(cross_bias.shape, f32),
-            jax.ShapeDtypeStruct((8, 128), f32),
+            jax.ShapeDtypeStruct((1, 128), f32),
         ),
         in_specs=[vmem] * 11,
         out_specs=(vmem,) * 4,
@@ -274,6 +469,22 @@
             sems,
             sems,
             sems,
+            grad_u,
+            grad_v,
+            grad_u,
+            grad_v,
+            grad_u,
+            grad_v,
+            rep_sems,
+            rep_sems,
+            rep_sems,
+            rep_sems,
+            pltpu.VMEM((8, 128), f32),
+            pltpu.SemaphoreType.DMA,
+            pltpu.SemaphoreType.DMA,
+            pltpu.VMEM((replicas, loops + 1, width), f32),
+            pltpu.SemaphoreType.DMA((replicas,)),
+            pltpu.SemaphoreType.DMA((replicas,)),
         ],
         compiler_params=pltpu.CompilerParams(
             collective_id=0, has_side_effects=True, vmem_limit_bytes=56 * 2**20
@@ -291,9 +502,7 @@
         debias_tower_bias[None, :],
         debias_output_weight[None, :],
     )
-    loss = lax.psum(loss[0, 0], ("section", "rep")) / total
-    gu, gv, gb = lax.psum((gu, gv, gb), "rep")
-    return (loss, gu.astype(f32), gv.astype(f32), gb)
+    return (loss[0, 0], gu.astype(f32)[:, None], gv.astype(f32)[:, None], gb)
 
 
 def solution(mesh):

time: 305 us -> 246 us (0.81)
  Pallas kernels: 127 us -> 237 us
  waiting for transfers between devices: 89.6 us -> 0 us
  blocking collectives: 65 us -> 0 us
  between operations: 15.8 us -> 1.83 us
    pallas_call x1, Pallas kernels: 127 us -> 237 us  [local(): pl.pallas_call(functools.partial(kernel, float(total)), out_shape=(jax.Sh...]
    psum x1 -> x0, waiting for transfers between devices: 89.5 us -> none  [local(): gu, gv, gb = lax.psum((gu, gv, gb), 'rep')]
    psum x2 -> x0, blocking collectives: 65 us -> none  [the longest x1 43.3 us: local(): loss = lax.psum(loss[0, 0], ('section', 'rep')) / total]
    convert_element_type x2 -> x0, other arithmetic: 6.62 us -> none  [local(): return (loss, gu.astype(f32), gv.astype(f32), gb)]
    unnamed x0 -> x2, other arithmetic: none -> 6.62 us
  transfers between devices with their start and end apart: 1 -> 0, of which waited for: 1 -> 0; matrix products, arithmetic and copies ran while one was open for 0% -> 0% of each run, Pallas kernels for 0% -> 0%
where the time goes in v2:
time: 246 us
  Pallas kernels  237 us (96%)
  other arithmetic  6.62 us (3%)
    pallas_call x1, Pallas kernels, local(): pl.pallas_call(functools.partial(kernel, float(total)), out_shape=(jax.Sh...  237 us
    unnamed x2, other arithmetic  6.62 us

profile of v2, /device:TPU:0, one launch (start us, length us, event | category | flops | bytes accessed | tf_op | source)
XLA Modules:
  0.0 246.0 jit_solution(16484321380786972644)
XLA Ops:
  0.6 237.0 %shard_map.138 = (bf16[2,2048,256]{2,1,0:T(8,128)(2,1)}, bf16[2,256,2048]{2,1,0:T(8,128)(2,1)}, f32[2,1,2048]{2,1,0:T(1,128)}, f32[1,128]{1,0:T(1,128)}) custom-call(bf16[8,32,2048]{2,1,0:T(8,128)(2,1)} %feat.1, s32[8,32]{1,0:T(8,128)} %pos.1, s32[8,32]{1,0:T(8,128)} %lab.1, bf16[2,1,2048,256]{3,2,1,0:T(8,128)(2,1)} %u.1, bf16[2,1,256,2048]{3,2,1,0:T(8,128)(2,1)} %v.1, ...), custom_call_target="tpu_custom_call" | custom-call | tf_op jit(solution)/shard_map/pallas_call | solution.py:445
  237.6 0.0 copy-start
  237.6 4.1 %bitcast_convert_fusion.1 = f32[2,1,2048,256]{3,2,1,0:T(8,128)} fusion(bf16[2,2048,256]{2,1,0:T(8,128)(2,1)} %get-tuple-element.9), kind=kLoop, calls=%fused_computation.1 | loop fusion | flops 1048576 | bytes 6291456
  241.7 0.0 copy-done
  241.7 0.0 copy-start.2
  241.7 0.0 copy-start.1
  241.7 2.5 %bitcast_convert_fusion = f32[2,1,256,2048]{3,2,1,0:T(8,128)} fusion(bf16[2,256,2048]{2,1,0:T(8,128)(2,1)S(1)} %copy-done), kind=kLoop, calls=%fused_computation | loop fusion | flops 1048576 | bytes 6291456
  244.2 0.0 copy-done.2
  244.3 0.0 copy-done.1
  244.3 0.6 copy.20
Async XLA Ops:
  237.6 4.1 %copy-start = (bf16[2,256,2048]{2,1,0:T(8,128)(2,1)S(1)}, bf16[2,256,2048]{2,1,0:T(8,128)(2,1)}, u32[]{:S(2)}) copy-start(bf16[2,256,2048]{2,1,0:T(8,128)(2,1)} %get-tuple-element.10) | copy-start | bytes 6291460
  241.7 2.5 %copy-start.2 = (f32[1,128]{1,0:T(1,128)S(1)}, f32[1,128]{1,0:T(1,128)}, u32[]{:S(2)}) copy-start(f32[1,128]{1,0:T(1,128)} %get-tuple-element.8) | copy-start | bytes 1540
  241.7 2.6 %copy-start.1 = (f32[2,1,2048]{2,1,0:T(1,128)S(1)}, f32[2,1,2048]{2,1,0:T(1,128)}, u32[]{:S(2)}) copy-start(f32[2,1,2048]{2,1,0:T(1,128)} %get-tuple-element.23) | copy-start | bytes 49156

commit v3 on v2

--- a/solution.py
+++ b/solution.py
@@ -286,8 +286,12 @@
             def _(kind=kind):
                 to_ends(kind, q).start()
 
-    def reduce_step(t):
-        @pl.when((t >= 1) & (t - 1 < pieces))
+    at_end = jnp.logical_not(has_outward | in_middle)
+
+    def reduce_step(t, ahead=False):
+        gathers = (t >= 1) & (t - 1 < pieces)
+
+        @pl.when(gathers & jnp.logical_not(at_end) if ahead else gathers)
         def _():
             gather_in(t - 1)
 
@@ -295,10 +299,22 @@
         def _():
             give_out(t - lag)
 
-    def weight_grads(slot):
-        part = 512
-        for c in range(width // part):
-            cols = slice(c * part, (c + 1) * part)
+    def send_ahead(start, stop):
+        @pl.when(at_end)
+        def _():
+            def one(q, carry):
+                for kind in range(2):
+                    to_middle(kind, q).start()
+                return carry
+
+            lax.fori_loop(start, stop, one, 0)
+
+    chunks = 4
+    chunk = width // chunks
+
+    def weight_grads(slot, then=None):
+        def some(c, carry):
+            cols = pl.ds(pl.multiple_of(c * chunk, chunk), chunk)
             own_u[slot, cols, :] = dot(normed[slot, :, cols], ginner[slot], TN).astype(
                 jnp.bfloat16
             )
@@ -307,6 +323,11 @@
             small[replica, slot : slot + 1, cols] = jnp.sum(
                 gc.astype(jnp.float32), axis=0, keepdims=True
             )
+            if then is not None:
+                then(c)
+            return carry
+
+        lax.fori_loop(0, chunks, some, 0)
 
     def loss_copy():
         return pltpu.make_async_remote_copy(
@@ -328,7 +349,7 @@
             device_id_type=MESH,
         )
 
-    beside = micro <= PARTS
+    beside = loops > 1 and micro + chunks <= PARTS
     for back in range(loops):
         slot = loops - 1 - back
 
@@ -361,17 +382,28 @@
             def _():
                 loss_copy().start()
 
-        weight_grads(slot)
-
+        if slot > 0:
+            weight_grads(slot)
+
+    now = (loops - 1) * micro if beside else 0
+    begin = max(now - 1, 0)
+    split = pieces - PARTS
+    send_ahead(begin, split)
+    if loops > 1:
+        weight_grads(0, lambda c: reduce_step(now + c, ahead=True))
+        now = now + chunks
+    else:
+        weight_grads(0)
+    send_ahead(split, pieces)
     small[replica, loops : loops + 1, :] = jnp.broadcast_to(loss_in[:1, :1], (1, width))
     for step in range(1, replicas):
         small_copy(replica, lax.rem(replica + step, replicas)).start()
 
     def tail(t, carry):
-        reduce_step(t)
+        reduce_step(t, ahead=True)
         return carry
 
-    lax.fori_loop((loops - 1) * micro if beside else 0, pieces + 5, tail, 0)
+    lax.fori_loop(now, pieces + 5, tail, 0)
 
     def drain(t, carry):
         slot, m = t // micro, t % micro

time: 246 us -> 239 us (0.972)
  Pallas kernels: 237 us -> 230 us
    pallas_call x1, Pallas kernels: 237 us -> 230 us  [local(): pl.pallas_call(functools.partial(kernel, float(total)), out_shape=(jax.Sh...]
where the time goes in v3:
time: 239 us
  Pallas kernels  230 us (96%)
  other arithmetic  6.62 us (3%)
    pallas_call x1, Pallas kernels, local(): pl.pallas_call(functools.partial(kernel, float(total)), out_shape=(jax.Sh...  230 us
    unnamed x2, other arithmetic  6.62 us

profile of v3, /device:TPU:0, one launch (start us, length us, event | category | flops | bytes accessed | tf_op | source)
XLA Modules:
  0.0 238.6 jit_solution(13304872055576315352)
XLA Ops:
  0.6 229.5 %shard_map.138 = (bf16[2,2048,256]{2,1,0:T(8,128)(2,1)}, bf16[2,256,2048]{2,1,0:T(8,128)(2,1)}, f32[2,1,2048]{2,1,0:T(1,128)}, f32[1,128]{1,0:T(1,128)}) custom-call(bf16[8,32,2048]{2,1,0:T(8,128)(2,1)} %feat.1, s32[8,32]{1,0:T(8,128)} %pos.1, s32[8,32]{1,0:T(8,128)} %lab.1, bf16[2,1,2048,256]{3,2,1,0:T(8,128)(2,1)} %u.1, bf16[2,1,256,2048]{3,2,1,0:T(8,128)(2,1)} %v.1, ...), custom_call_target="tpu_custom_call" | custom-call | tf_op jit(solution)/shard_map/pallas_call | solution.py:477
  230.2 0.0 copy-start
  230.2 4.1 %bitcast_convert_fusion.1 = f32[2,1,2048,256]{3,2,1,0:T(8,128)} fusion(bf16[2,2048,256]{2,1,0:T(8,128)(2,1)} %get-tuple-element.9), kind=kLoop, calls=%fused_computation.1 | loop fusion | flops 1048576 | bytes 6291456
  234.3 0.0 copy-done
  234.3 0.0 copy-start.2
  234.3 0.0 copy-start.1
  234.3 2.5 %bitcast_convert_fusion = f32[2,1,256,2048]{3,2,1,0:T(8,128)} fusion(bf16[2,256,2048]{2,1,0:T(8,128)(2,1)S(1)} %copy-done), kind=kLoop, calls=%fused_computation | loop fusion | flops 1048576 | bytes 6291456
  236.8 0.0 copy-done.2
  236.9 0.0 copy-done.1
  236.9 0.6 copy.20
Async XLA Ops:
  230.2 4.1 %copy-start = (bf16[2,256,2048]{2,1,0:T(8,128)(2,1)S(1)}, bf16[2,256,2048]{2,1,0:T(8,128)(2,1)}, u32[]{:S(2)}) copy-start(bf16[2,256,2048]{2,1,0:T(8,128)(2,1)} %get-tuple-element.10) | copy-start | bytes 6291460
  234.3 2.5 %copy-start.2 = (f32[1,128]{1,0:T(1,128)S(1)}, f32[1,128]{1,0:T(1,128)}, u32[]{:S(2)}) copy-start(f32[1,128]{1,0:T(1,128)} %get-tuple-element.8) | copy-start | bytes 1540
  234.3 2.6 %copy-start.1 = (f32[2,1,2048]{2,1,0:T(1,128)S(1)}, f32[2,1,2048]{2,1,0:T(1,128)}, u32[]{:S(2)}) copy-start(f32[2,1,2048]{2,1,0:T(1,128)} %get-tuple-element.23) | copy-start | bytes 49156

commit v4 on v3

--- a/solution.py
+++ b/solution.py
@@ -220,7 +220,9 @@
     pieces = loops * PARTS
     rank = own_v.shape[1]
     tall_u, tall_v = width // PARTS, rank // PARTS
-    lag = jnp.where(in_middle, 3, 5)
+    at_end = jnp.logical_not(has_outward | in_middle)
+    early = jnp.where(at_end, 1, 2)
+    lag = jnp.where(in_middle, 6, 9)
 
     def piece(ref, kind, q):
         tall = (tall_u, tall_v)[kind]
@@ -286,14 +288,12 @@
             def _(kind=kind):
                 to_ends(kind, q).start()
 
-    at_end = jnp.logical_not(has_outward | in_middle)
-
     def reduce_step(t, ahead=False):
-        gathers = (t >= 1) & (t - 1 < pieces)
+        gathers = (t >= early) & (t - early < pieces)
 
         @pl.when(gathers & jnp.logical_not(at_end) if ahead else gathers)
         def _():
-            gather_in(t - 1)
+            gather_in(t - early)
 
         @pl.when((t >= lag) & (t - lag < pieces))
         def _():
@@ -403,7 +403,7 @@
         reduce_step(t, ahead=True)
         return carry
 
-    lax.fori_loop(now, pieces + 5, tail, 0)
+    lax.fori_loop(now, pieces + 9, tail, 0)
 
     def drain(t, carry):
         slot, m = t // micro, t % micro

time: 239 us -> 241 us (level)
  no operation moved by 1% of the time
where the time goes in v4:
time: 241 us; the launch traced here: 240 us
  Pallas kernels  231 us (96%)
  other arithmetic  6.62 us (3%)
    pallas_call x1, Pallas kernels, local(): pl.pallas_call(functools.partial(kernel, float(total)), out_shape=(jax.Sh...  231 us
    unnamed x2, other arithmetic  6.62 us

profile of v4, /device:TPU:0, one launch (start us, length us, event | category | flops | bytes accessed | tf_op | source)
XLA Modules:
  0.0 240.5 jit_solution(7522574931103388482)
XLA Ops:
  0.6 231.4 %shard_map.138 = (bf16[2,2048,256]{2,1,0:T(8,128)(2,1)}, bf16[2,256,2048]{2,1,0:T(8,128)(2,1)}, f32[2,1,2048]{2,1,0:T(1,128)}, f32[1,128]{1,0:T(1,128)}) custom-call(bf16[8,32,2048]{2,1,0:T(8,128)(2,1)} %feat.1, s32[8,32]{1,0:T(8,128)} %pos.1, s32[8,32]{1,0:T(8,128)} %lab.1, bf16[2,1,2048,256]{3,2,1,0:T(8,128)(2,1)} %u.1, bf16[2,1,256,2048]{3,2,1,0:T(8,128)(2,1)} %v.1, ...), custom_call_target="tpu_custom_call" | custom-call | tf_op jit(solution)/shard_map/pallas_call | solution.py:477
  232.0 0.0 copy-start
  232.1 4.1 %bitcast_convert_fusion.1 = f32[2,1,2048,256]{3,2,1,0:T(8,128)} fusion(bf16[2,2048,256]{2,1,0:T(8,128)(2,1)} %get-tuple-element.9), kind=kLoop, calls=%fused_computation.1 | loop fusion | flops 1048576 | bytes 6291456
  236.1 0.0 copy-done
  236.1 0.0 copy-start.2
  236.1 0.0 copy-start.1
  236.2 2.5 %bitcast_convert_fusion = f32[2,1,256,2048]{3,2,1,0:T(8,128)} fusion(bf16[2,256,2048]{2,1,0:T(8,128)(2,1)S(1)} %copy-done), kind=kLoop, calls=%fused_computation | loop fusion | flops 1048576 | bytes 6291456
  238.7 0.0 copy-done.2
  238.7 0.0 copy-done.1
  238.7 0.6 copy.20
Async XLA Ops:
  232.0 4.1 %copy-start = (bf16[2,256,2048]{2,1,0:T(8,128)(2,1)S(1)}, bf16[2,256,2048]{2,1,0:T(8,128)(2,1)}, u32[]{:S(2)}) copy-start(bf16[2,256,2048]{2,1,0:T(8,128)(2,1)} %get-tuple-element.10) | copy-start | bytes 6291460
  236.1 2.5 %copy-start.2 = (f32[1,128]{1,0:T(1,128)S(1)}, f32[1,128]{1,0:T(1,128)}, u32[]{:S(2)}) copy-start(f32[1,128]{1,0:T(1,128)} %get-tuple-element.8) | copy-start | bytes 1540
  236.1 2.6 %copy-start.1 = (f32[2,1,2048]{2,1,0:T(1,128)S(1)}, f32[2,1,2048]{2,1,0:T(1,128)}, u32[]{:S(2)}) copy-start(f32[2,1,2048]{2,1,0:T(1,128)} %get-tuple-element.23) | copy-start | bytes 49156
